TPU v7x, 32 devices: a whole 2x2x4 slice. The times are simulated.
32 devices in a mesh: wide: 8 (over y, x, core), narrow: 4 (over z).
Axes of the slice: x: 2, y: 2, z: 4, core: 2. Of those that a mesh axis runs over, the one named last changes fastest.
Arguments:
- tokens: bfloat16 [128, 128, 1536], P('wide'), may hold values from -8 to 8
- ln_gain: bfloat16 [1536], replicated, may hold values from 0.3984375 to 1.59375
- gate_weight: bfloat16 [1536, 8960], P(None, 'narrow'), may hold values from -0.15625 to 0.15625
- up_weight: bfloat16 [1536, 8960], P(None, 'narrow'), may hold values from -0.15625 to 0.15625
- down_weight: bfloat16 [8960, 1536], P('narrow'), may hold values from -0.0625 to 0.0625
- out_gain: bfloat16 [1536], replicated, may hold values from 0.25 to 1.75
- shard_ids: int32 [128], P('wide'), may hold values from 0 to 7, as said below
- slab_old: bfloat16 [65536, 1536], P(('wide', 'narrow')), may hold values from -8 to 8
- queries: bfloat16 [8, 64, 1536], P('wide'), may hold values from -12 to 12
- positives: int32 [8, 64], P('wide'), may hold values from 0 to 65663
- owners: int32 [4], replicated, may hold values from 0 to 7
Outputs:
- index_new: bfloat16 [8, 8, 4, 1536], P('wide', 'narrow')
- losses: float32 [4, 64], replicated
Inputs may be any that keep to these rules, and one draw needn't show every extreme that they name: `shard_ids`: among the 16 passages of one index of wide at most 4 have the same shard id; in every draw one shard id is held by exactly 4 passages of every index of wide.
All inputs are finite; a program needn't handle non-finite values.
Results may differ from a plain program's by a relative error of at most 0.0029.
Values may be sent and summed in bfloat16 or wider, within the bound.
A program may use at most 128 MiB of HBM per device.

v0:
```python
import math

import jax
import jax.numpy as jnp
from jax import lax
from jax.sharding import PartitionSpec as P

EPS = 1e-06


def rms_scale(values):
    return lax.rsqrt(jnp.mean(values * values, axis=-1, keepdims=True) + EPS)


def local(
    tokens,
    ln_gain,
    gate_weight,
    up_weight,
    down_weight,
    out_gain,
    shard_ids,
    slab_old,
    queries,
    positives,
    owners,
):
    passages, seq_len, width = tokens.shape
    narrow_count = lax.axis_size("narrow")
    wide_count = lax.axis_size("wide")
    narrow_rank = lax.axis_index("narrow")
    wide_rank = lax.axis_index("wide")
    piece_width = width // narrow_count
    capacity = 2 * passages // wide_count
    values = tokens.astype(jnp.float32)
    normed = (values * rms_scale(values) * ln_gain.astype(jnp.float32)).astype(jnp.bfloat16)
    normed = normed.reshape(passages * seq_len, width)
    gate = jnp.dot(normed, gate_weight, preferred_element_type=jnp.float32)
    upward = jnp.dot(normed, up_weight, preferred_element_type=jnp.float32)
    hidden = (jax.nn.silu(gate) * upward).astype(jnp.bfloat16)
    partial_value = jnp.dot(hidden, down_weight, preferred_element_type=jnp.float32)
    pooled_part = jnp.mean(partial_value.reshape(passages, seq_len, width), axis=1)
    token_mean = jnp.mean(values, axis=1)
    offset = narrow_rank * piece_width
    pooled = lax.psum(pooled_part, "narrow") + token_mean
    norm_scale = rms_scale(pooled)
    own_piece = lax.dynamic_slice_in_dim(pooled, offset, piece_width, 1)
    gain_piece = lax.dynamic_slice_in_dim(out_gain.astype(jnp.float32), offset, piece_width, 0)
    embedding = (own_piece * norm_scale * gain_piece).astype(jnp.bfloat16)
    positions = jnp.arange(passages, dtype=jnp.int32)
    earlier = positions[:, None] > positions[None, :]
    same = shard_ids[:, None] == shard_ids[None, :]
    rank = jnp.sum((earlier & same).astype(jnp.int32), axis=1)
    slots = shard_ids * capacity + rank
    dispatch = slots[None, :] == jnp.arange(wide_count * capacity, dtype=jnp.int32)[:, None]
    outgoing = jnp.dot(dispatch.astype(jnp.bfloat16), embedding, preferred_element_type=jnp.float32)
    outgoing = outgoing.astype(jnp.bfloat16).reshape(wide_count, capacity, piece_width)
    numbers = wide_rank * passages + positions
    slot_numbers = jnp.sum(jnp.where(dispatch, numbers[None, :] + 1, 0), axis=1) - 1
    slot_numbers = slot_numbers.reshape(wide_count, capacity, 1)
    arrived, arrived_numbers = (
        lax.all_to_all(
            lax.all_to_all(outgoing, "wide", split_axis=0, concat_axis=0, tiled=True),
            "narrow",
            split_axis=0,
            concat_axis=2,
            tiled=True,
        ),
        lax.all_to_all(
            lax.all_to_all(slot_numbers, "wide", split_axis=0, concat_axis=0, tiled=True),
            "narrow",
            split_axis=0,
            concat_axis=2,
            tiled=True,
        ),
    )
    old_total = slab_old.shape[0] * wide_count * narrow_count
    new_rows = arrived.reshape(-1, width)
    new_numbers = arrived_numbers[:, :, 0].reshape(-1)
    valid = (new_numbers >= 0)[None, :]
    new_global = old_total + new_numbers
    device_linear = wide_rank * narrow_count + narrow_rank
    old_global = device_linear * slab_old.shape[0] + jnp.arange(slab_old.shape[0], dtype=jnp.int32)
    scale = 1.0 / math.sqrt(width)
    contract = (((1,), (1,)), ((), ()))
    block_size = queries.shape[1]
    step_count = owners.shape[0]
    mine = owners == wide_rank
    own_blocks = jnp.where(mine[:, None, None], queries[0].astype(jnp.float32)[None], 0.0)
    own_positives = jnp.where(mine[:, None], positives[0].astype(jnp.float32)[None], 0.0)
    summed_blocks, summed_positives = lax.psum((own_blocks, own_positives), "wide")
    blocks = summed_blocks.astype(jnp.bfloat16).reshape(step_count * block_size, width)
    chosen = summed_positives.astype(jnp.int32).reshape(step_count * block_size)
    old_scores = (
        lax.dot_general(blocks, slab_old, contract, preferred_element_type=jnp.float32) * scale
    )
    new_scores = (
        lax.dot_general(blocks, new_rows, contract, preferred_element_type=jnp.float32) * scale
    )
    masked = jnp.where(valid, new_scores, -jnp.inf)
    local_max = jnp.maximum(jnp.max(old_scores, axis=1), jnp.max(masked, axis=1))
    hit_old = old_global[None, :] == chosen[:, None]
    hit_new = valid & (new_global[None, :] == chosen[:, None])
    local_positive = jnp.sum(jnp.where(hit_old, old_scores, 0.0), axis=1) + jnp.sum(
        jnp.where(hit_new, new_scores, 0.0), axis=1
    )
    largest = lax.pmax(local_max, ("wide", "narrow"))
    local_total = jnp.sum(jnp.exp(old_scores - largest[:, None]), axis=1)
    local_total = local_total + jnp.sum(
        jnp.where(valid, jnp.exp(new_scores - largest[:, None]), 0.0), axis=1
    )
    total, picked = lax.psum((local_total, local_positive), ("wide", "narrow"))
    losses = (largest + jnp.log(total) - picked).reshape(step_count, block_size)
    return (arrived[None], losses)


def solution(mesh):
    return jax.shard_map(
        local,
        mesh=mesh,
        in_specs=(
            P("wide", None, None),
            P(),
            P(None, "narrow"),
            P(None, "narrow"),
            P("narrow", None),
            P(),
            P("wide"),
            P(("wide", "narrow"), None),
            P("wide", None, None),
            P("wide", None),
            P(),
        ),
        out_specs=(P("wide", "narrow", None, None), P()),
        check_vma=False,
    )
```

profile of v0, /device:TPU:0, one launch (start us, length us, event | category | flops | bytes accessed | tf_op | source)
XLA Modules:
  0.0 260.1 jit_solution(12697196539103619592)
XLA Ops:
  7.2 0.8 convert_element_type.39
  8.1 5.4 %convert_reduce_fusion = (f32[16,1536]{1,0:T(8,128)}, f32[16,128]{1,0:T(8,128)S(1)}) fusion(bf16[16,128,1536]{2,1,0:T(8,128)(2,1)} %param.11), kind=kLoop, calls=%fused_computation | loop fusion | flops 12556288 | bytes 6397952 | tf_op jit(solution)/shard_map/reduce_sum | solution.py:43
  13.5 1.5 fusion.2
  15.0 2.6 copy-done.1
  17.6 18.6 %fusion.12 = f32[2048,2240]{0,1:T(8,128)} fusion(bf16[2048,1536]{1,0:T(8,128)(2,1)S(1)} %bitcast.29, bf16[1536,2240]{0,1:T(8,128)(2,1)} %param.13), kind=kOutput, calls=%fused_computation.49 | convolution fusion | flops 14092861440 | bytes 31522816 | tf_op jit(solution)/shard_map/dot_general | solution.py:38
  36.2 39.4 %bitcast_reduce_fusion = f32[16,1536]{1,0:T(8,128)S(1)} fusion(bf16[2240,1536]{1,0:T(8,128)(2,1)} %param.15, f32[2048,2240]{0,1:T(8,128)} %fusion.12, bf16[2048,1536]{1,0:T(8,128)(2,1)} %bitcast.30, bf16[1536,2240]{0,1:T(8,128)(2,1)} %param.14), kind=kOutput, calls=%fused_computation.7 | convolution fusion | flops 28216369152 | bytes 38502400 | tf_op jit(solution)/shard_map/dot_general | solution.py:41
  75.7 0.6 broadcast_multiply_fusion
  76.3 0.2 convert_reduce_fusion.1
  76.6 0.7 sub.26
  77.3 5.2 %all-to-all-start.2 = ((s32[8,4,1]{1,2,0:T(1,128)}), s32[8,4,1]{1,2,0:T(1,128)}, u32[]{:S(2)}, u32[]{:S(2)}) async-start(s32[8,4,1]{1,2,0:T(1,128)} %bitcast.6), calls=%async_computation.2 | async-start | bytes 8192 | tf_op jit(solution)/shard_map/all_to_all | solution.py:70
  82.6 0.2 broadcast_select_fusion
  82.9 54.1 %all-reduce.6 = (bf16[4,64,1536]{2,1,0:T(8,128)(2,1)S(1)}, f32[4,64]{1,0:T(4,128)S(1)}) all-reduce(f32[4,64,1536]{2,1,0:T(8,128)S(1)} %broadcast_select_fusion, f32[4,64]{1,0:T(4,128)S(1)} %broadcast_select_fusion.1), channel_id=1, replica_groups=mesh['wide'=8,'narrow'=4] {'wide'}, use_global_device_ids=true, to_apply=%region_6.7 | all-reduce | flops 393472 | bytes 2361344 | tf_op jit(solution)/shard_map/psum | solution.py:91
  137.0 4.7 %fusion.11 = (f32[256]{0:T(256)S(1)}, f32[256,2048]{1,0:T(8,128)S(1)}) fusion(bf16[256,1536]{1,0:T(8,128)(2,1)S(1)} %bitcast.31, bf16[2048,1536]{1,0:T(8,128)(2,1)} %param.18), kind=kOutput, calls=%fused_computation.48 | convolution fusion | flops 1611661056 | bytes 9176064 | tf_op jit(solution)/shard_map/dot_general | solution.py:95
  141.7 0.8 dynamic-slice_convert_fusion
  142.4 4.8 %all-to-all-start.3 = ((s32[8,4,1]{1,2,0:T(1,128)}), s32[8,4,1]{1,2,0:T(1,128)S(1)}, u32[]{:S(2)}, u32[]{:S(2)}) async-start(s32[8,4,1]{1,2,0:T(1,128)} %all-to-all-done.2), calls=%async_computation.3 | async-start | bytes 8192 | tf_op jit(solution)/shard_map/all_to_all | solution.py:69
  147.3 5.5 %all-to-all-done.3 = s32[8,4,1]{1,2,0:T(1,128)S(1)} async-done(((s32[8,4,1]{1,2,0:T(1,128)}), s32[8,4,1]{1,2,0:T(1,128)S(1)}, u32[]{:S(2)}, u32[]{:S(2)}) %all-to-all-start.3) | async-done | bytes 160 | tf_op jit(solution)/shard_map/all_to_all | solution.py:69
  152.8 0.1 copy.22
  152.9 1.0 multiply_reduce_fusion
  154.0 0.3 convolution_convert_fusion
  154.2 0.6 reshape.88
  154.9 4.0 %all-to-all-start = ((bf16[8,4,384]{2,1,0:T(4,128)(2,1)}), bf16[8,4,384]{2,1,0:T(4,128)(2,1)}, u32[]{:S(2)}, u32[]{:S(2)}) async-start(bf16[8,4,384]{2,1,0:T(4,128)(2,1)} %reshape.88), calls=%async_computation | async-start | bytes 49152 | tf_op jit(solution)/shard_map/all_to_all | solution.py:63
  158.8 0.1 compare_reduce_fusion
  159.0 4.7 %all-to-all-done = bf16[8,4,384]{2,1,0:T(4,128)(2,1)} async-done(((bf16[8,4,384]{2,1,0:T(4,128)(2,1)}), bf16[8,4,384]{2,1,0:T(4,128)(2,1)}, u32[]{:S(2)}, u32[]{:S(2)}) %all-to-all-start) | async-done | bytes 24608 | tf_op jit(solution)/shard_map/all_to_all | solution.py:63
  163.6 3.3 %all-to-all-start.1 = ((bf16[8,4,384]{2,1,0:T(4,128)(2,1)}), bf16[8,4,384]{2,1,0:T(4,128)(2,1)S(1)}, u32[]{:S(2)}, u32[]{:S(2)}) async-start(bf16[8,4,384]{2,1,0:T(4,128)(2,1)} %all-to-all-done), calls=%async_computation.1 | async-start | bytes 49152 | tf_op jit(solution)/shard_map/all_to_all | solution.py:62
  166.9 0.1 add_reduce_fusion
  167.2 5.3 %all-to-all-done.1 = bf16[8,4,384]{2,1,0:T(4,128)(2,1)S(1)} async-done(((bf16[8,4,384]{2,1,0:T(4,128)(2,1)}), bf16[8,4,384]{2,1,0:T(4,128)(2,1)S(1)}, u32[]{:S(2)}, u32[]{:S(2)}) %all-to-all-start.1) | async-done | bytes 24608 | tf_op jit(solution)/shard_map/all_to_all | solution.py:62
  172.5 0.6 broadcast_in_dim.106
  173.2 0.3 select_reduce_fusion.3
  173.5 38.4 %pmax.7 = f32[256]{0:T(256)S(1)} all-reduce(f32[256]{0:T(256)S(1)} %max.5), channel_id=1, replica_groups=mesh['wide'=8,'narrow'=4] {'wide','narrow'}, use_global_device_ids=true, to_apply=%region_10.11 | all-reduce | flops 256 | bytes 2048 | tf_op jit(solution)/shard_map/pmax | solution.py:107
  211.9 0.6 exponential_reduce_fusion
  212.7 39.9 %all-reduce = (f32[256]{0:T(256)S(1)}, f32[256]{0:T(256)S(1)}) all-reduce(f32[256]{0:T(256)S(1)} %add.119, f32[256]{0:T(256)S(1)} %add.112), channel_id=1, replica_groups=mesh['wide'=8,'narrow'=4] {'wide','narrow'}, use_global_device_ids=true, to_apply=%region_17.18 | all-reduce | flops 512 | bytes 4096 | tf_op jit(solution)/shard_map/psum | solution.py:112
  252.5 0.7 reshape.91
  (39 shorter events, 0.7 us)
Async XLA Ops:
  7.2 145.8 %all-reduce.5.cloned.1.call-start = ((), (), s32[]{:S(2)}) async-start(), calls=%async_computation.4 | async-start | bytes 196608 | tf_op jit(solution)/shard_map/psum | solution.py:45
  7.2 6.3 %copy-start = (bf16[16,128,1536]{2,1,0:T(8,128)(2,1)S(1)}, bf16[16,128,1536]{2,1,0:T(8,128)(2,1)}, u32[]{:S(2)}) copy-start(bf16[16,128,1536]{2,1,0:T(8,128)(2,1)} %param.11) | copy-start | bytes 18874372
  15.0 2.6 %copy-start.1 = (bf16[16,128,1536]{2,1,0:T(8,128)(2,1)}, bf16[16,128,1536]{2,1,0:T(8,128)(2,1)S(1)}, u32[]{:S(2)}) copy-start(bf16[16,128,1536]{2,1,0:T(8,128)(2,1)S(1)} %fusion.2) | copy-start | bytes 18874372
  36.2 40.1 %copy-start.4 = (s32[16]{0:T(128)S(1)}, s32[16]{0:T(128)}, u32[]{:S(2)}) copy-start(s32[16]{0:T(128)} %param.17) | copy-start | bytes 196
  36.2 46.3 %copy-start.3 = (bf16[1,64,1536]{2,1,0:T(8,128)(2,1)S(1)}, bf16[1,64,1536]{2,1,0:T(8,128)(2,1)}, u32[]{:S(2)}) copy-start(bf16[1,64,1536]{2,1,0:T(8,128)(2,1)} %param.19) | copy-start | bytes 589828
  36.2 46.3 %copy-start.5 = (s32[4]{0:T(128)S(1)}, s32[4]{0:T(128)}, u32[]{:S(2)}) copy-start(s32[4]{0:T(128)} %param.21) | copy-start | bytes 52
  36.2 46.6 %copy-start.6 = (s32[1,64]{1,0:T(1,128)S(1)}, s32[1,64]{1,0:T(1,128)}, u32[]{:S(2)}) copy-start(s32[1,64]{1,0:T(1,128)} %param.20) | copy-start | bytes 772
  77.3 65.1 %all-to-all-start.2 = ((s32[8,4,1]{1,2,0:T(1,128)}), s32[8,4,1]{1,2,0:T(1,128)}, u32[]{:S(2)}, u32[]{:S(2)}) async-start(s32[8,4,1]{1,2,0:T(1,128)} %bitcast.6), calls=%async_computation.2 | async-start | bytes 8192 | tf_op jit(solution)/shard_map/all_to_all | solution.py:70
  82.6 70.4 %copy-start.2 = (f32[16,1536]{1,0:T(8,128)S(1)}, f32[16,1536]{1,0:T(8,128)}, u32[]{:S(2)}) copy-start(f32[16,1536]{1,0:T(8,128)} %get-tuple-element.2) | copy-start | bytes 294916
  142.4 10.4 %all-to-all-start.3 = ((s32[8,4,1]{1,2,0:T(1,128)}), s32[8,4,1]{1,2,0:T(1,128)S(1)}, u32[]{:S(2)}, u32[]{:S(2)}) async-start(s32[8,4,1]{1,2,0:T(1,128)} %all-to-all-done.2), calls=%async_computation.3 | async-start | bytes 8192 | tf_op jit(solution)/shard_map/all_to_all | solution.py:69
  154.9 8.8 %all-to-all-start = ((bf16[8,4,384]{2,1,0:T(4,128)(2,1)}), bf16[8,4,384]{2,1,0:T(4,128)(2,1)}, u32[]{:S(2)}, u32[]{:S(2)}) async-start(bf16[8,4,384]{2,1,0:T(4,128)(2,1)} %reshape.88), calls=%async_computation | async-start | bytes 49152 | tf_op jit(solution)/shard_map/all_to_all | solution.py:63
  163.6 8.9 %all-to-all-start.1 = ((bf16[8,4,384]{2,1,0:T(4,128)(2,1)}), bf16[8,4,384]{2,1,0:T(4,128)(2,1)S(1)}, u32[]{:S(2)}, u32[]{:S(2)}) async-start(bf16[8,4,384]{2,1,0:T(4,128)(2,1)} %all-to-all-done), calls=%async_computation.1 | async-start | bytes 49152 | tf_op jit(solution)/shard_map/all_to_all | solution.py:62
Sparse Core Ops, SparseCore 0:
  76.4 36.9 all-reduce.4
where the time goes:
time: 261 us; the launch traced here: 260 us
  blocking collectives  132 us (51%)
  matrix products  63.3 us (24%)
  starting transfers between devices  17.3 us (7%)
  waiting for transfers between devices  15.5 us (6%)
  between operations  14.2 us (5%)
  other arithmetic  11.8 us (5%)
  local copies, waits for them, and re-layouts  5.57 us (2%)
    psum x1, blocking collectives, local(): lax.psum((own_blocks, own_positives), 'wide')  54.1 us
    psum x1, blocking collectives, local(): total, picked = lax.psum((local_total, local_positive), ('wide', 'narrow'))  39.9 us
    dot_general x1, matrix products, local(): jnp.dot(hidden, down_weight, preferred_element_type=jnp.float32)  39.4 us
    pmax x1, blocking collectives, local(): largest = lax.pmax(local_max, ('wide', 'narrow'))  38.4 us
    dot_general x1, matrix products, local(): gate = jnp.dot(normed, gate_weight, preferred_element_type=jnp.float32)  18.6 us
    all_to_all x1, waiting for transfers between devices, local(): lax.all_to_all(lax.all_to_all(slot_numbers, 'wide', split_axis=0, concat_...  5.49 us
    reduce_sum x1, other arithmetic, local(): token_mean = jnp.mean(values, axis=1)  5.4 us
    all_to_all x1, waiting for transfers between devices, local(): lax.all_to_all(lax.all_to_all(outgoing, 'wide', split_axis=0, concat_axis...  5.29 us
  transfers between devices with their start and end apart: 5, of which 3 were waited for; matrix products, arithmetic and copies ran while one was open for 3% of the time, Pallas kernels for 0%

commit v1 on v0

v1 whole, which is shorter than its diff:
```python
import functools
import math

import jax
import jax.numpy as jnp
from jax import lax
from jax.experimental import pallas as pl
from jax.experimental.pallas import tpu as pltpu
from jax.sharding import PartitionSpec as P

EPS = 1e-06
MESH = pl.DeviceIdType.MESH
CHUNK = 256
ROWS = 256
SPLIT = 4
LOADS = 4
MSG = 16


def kernel(
    dims,
    tokens_ref,
    gain_ref,
    gate_ref,
    up_ref,
    down_ref,
    out_gain_ref,
    place_ref,
    slab_ref,
    queries_ref,
    positives_ref,
    owners_ref,
    index_ref,
    losses_ref,
    x_ref,
    gate_v,
    up_v,
    down_v,
    slab_v,
    q_all,
    p_all,
    blocks,
    hidden_sum,
    token_mean,
    total,
    part,
    part_in,
    messages,
    messages_in,
    stats,
    x_sem,
    w_sem,
    big_sem,
    own_sem,
    q_send,
    q_recv,
    p_send,
    p_recv,
    part_send,
    part_recv,
    msg_send,
    msg_recv,
    stat_send,
    stat_recv,
):
    passages, seq, wide_count, narrow_count, steps, block = dims
    width = tokens_ref.shape[1]
    units = gate_ref.shape[1]
    full, tail = units // CHUNK, units % CHUNK
    per = passages // narrow_count
    groups = 8 // per
    lanes = width // groups
    sources = wide_count // narrow_count
    devices = wide_count * narrow_count
    count = steps * block
    w = lax.axis_index("wide")
    n = lax.axis_index("narrow")
    me = w * narrow_count + n

    def token_copy(i):
        rows = pl.ds(pl.multiple_of(i * seq, seq), seq)
        return pltpu.make_async_copy(tokens_ref.at[rows, :], x_ref.at[rows, :], x_sem.at[i])

    def weight_copies(c):
        rows = pl.ds(pl.multiple_of(c * (width // LOADS), width // LOADS), width // LOADS)
        return (
            pltpu.make_async_copy(gate_ref.at[rows, :], gate_v.at[rows, :], w_sem.at[0, c]),
            pltpu.make_async_copy(up_ref.at[rows, :], up_v.at[rows, :], w_sem.at[1, c]),
        )

    down_copy = pltpu.make_async_copy(down_ref, down_v, big_sem.at[0])
    slab_copy = pltpu.make_async_copy(slab_ref, slab_v, big_sem.at[1])
    own_q = pltpu.make_async_copy(queries_ref, q_all.at[w], own_sem.at[0])
    own_p = pltpu.make_async_copy(positives_ref, p_all.at[w], own_sem.at[1])

    @pl.loop(0, passages)
    def _(i):
        token_copy(i).start()

    @pl.loop(0, LOADS)
    def _(c):
        for copy in weight_copies(c):
            copy.start()

    down_copy.start()
    slab_copy.start()
    own_q.start()
    own_p.start()

    barrier = pltpu.get_barrier_semaphore()

    @pl.loop(1, devices)
    def _(k):
        other = lax.rem(me + k, devices)
        pl.semaphore_signal(
            barrier,
            inc=1,
            device_id=(other // narrow_count, lax.rem(other, narrow_count)),
            device_id_type=MESH,
        )

    gain = gain_ref[...]

    @pl.loop(0, passages)
    def _(i):
        token_copy(i).wait()
        rows = pl.ds(pl.multiple_of(i * seq, seq), seq)
        values = x_ref[rows, :].astype(jnp.float32)
        scale = lax.rsqrt(jnp.mean(values * values, axis=1, keepdims=True) + EPS)
        token_mean[pl.ds(i, 1), :] = jnp.sum(values, axis=0, keepdims=True) * (1.0 / seq)
        x_ref[rows, :] = (values * scale * gain).astype(jnp.bfloat16)

    pl.semaphore_wait(barrier, devices - 1)

    def query_copies(owner, target):
        return (
            pltpu.make_async_remote_copy(
                src_ref=queries_ref,
                dst_ref=q_all.at[owner],
                send_sem=q_send.at[target],
                recv_sem=q_recv.at[owner],
                device_id=(target, n),
                device_id_type=MESH,
            ),
            pltpu.make_async_remote_copy(
                src_ref=positives_ref,
                dst_ref=p_all.at[owner],
                send_sem=p_send.at[target],
                recv_sem=p_recv.at[owner],
                device_id=(target, n),
                device_id_type=MESH,
            ),
        )

    @pl.loop(1, wide_count)
    def _(k):
        for copy in query_copies(w, lax.rem(w + k, wide_count)):
            copy.start()

    def encode(c, size):
        cols = pl.ds(pl.multiple_of(c * CHUNK, CHUNK), size)
        held = ROWS // seq
        for i in range(passages // held):
            x = x_ref[i * ROWS : (i + 1) * ROWS, :]
            gate = jnp.dot(x, gate_v[:, cols], preferred_element_type=jnp.float32)
            upward = jnp.dot(x, up_v[:, cols], preferred_element_type=jnp.float32)
            hidden = gate * upward * (1.0 + jnp.tanh(0.5 * gate))
            summed = jnp.sum(hidden.reshape(held, seq, size), axis=1)
            hidden_sum[c, i * held : (i + 1) * held, :size] = summed * (0.5 / seq)

    def project(c, size):
        mean = hidden_sum[c, :, :size]
        high = mean.astype(jnp.bfloat16)
        low = (mean - high.astype(jnp.float32)).astype(jnp.bfloat16)
        rows = pl.ds(pl.multiple_of(c * CHUNK, CHUNK), size)
        total[...] += jnp.dot(
            jnp.concatenate([high, low], axis=0),
            down_v[rows, :],
            preferred_element_type=jnp.float32,
        )

    total[...] = jnp.zeros_like(total)

    @pl.loop(0, LOADS)
    def _(c):
        for copy in weight_copies(c):
            copy.wait()

    encode(0, CHUNK)
    down_copy.wait()

    @pl.loop(1, full)
    def _(c):
        project(c - 1, CHUNK)
        encode(c, CHUNK)

    project(full - 1, CHUNK)
    if tail:
        encode(full, tail)
        project(full, tail)

    branch = total[:passages, :] + total[passages:, :] + token_mean[...] * (1.0 / narrow_count)
    for j in range(narrow_count):
        for g in range(groups):
            part[j, g * per : (g + 1) * per, :] = branch[
                j * per : (j + 1) * per, g * lanes : (g + 1) * lanes
            ]

    def part_copy(sender, target):
        return pltpu.make_async_remote_copy(
            src_ref=part.at[target],
            dst_ref=part_in.at[sender],
            send_sem=part_send.at[target],
            recv_sem=part_recv.at[sender],
            device_id=(w, target),
            device_id_type=MESH,
        )

    for k in range(1, narrow_count):
        part_copy(n, lax.rem(n + k, narrow_count)).start()

    own_q.wait()
    own_p.wait()

    @pl.loop(1, wide_count)
    def _(k):
        for copy in query_copies(lax.rem(w + k, wide_count), w):
            copy.wait_recv()

    lane = lax.broadcasted_iota(jnp.int32, (1, 128), 1)
    pieces = []
    for t in range(steps):
        blocks[t * block : (t + 1) * block, :] = q_all[owners_ref[t]]
    for t in range(0, steps, 2):
        pieces.append(
            jnp.where(
                lane < block,
                p_all[owners_ref[t]][0:1, :],
                p_all[owners_ref[t + 1]][0:1, :],
            )
        )
    chosen = jnp.concatenate(pieces, axis=1)
    factor = 1.0 / math.sqrt(width)
    contract = (((1,), (1,)), ((), ()))
    slab_copy.wait()
    old_rows = slab_ref.shape[0]
    tile = 512

    def old_tile(i, carry):
        top, mass, picked = carry
        rows = pl.ds(pl.multiple_of(i * tile, tile), tile)
        scores = factor * lax.dot_general(
            slab_v[rows, :], blocks[...], contract, preferred_element_type=jnp.float32
        )
        numbers = me * old_rows + i * tile + lax.broadcasted_iota(jnp.int32, (tile, 1), 0)
        picked += jnp.sum(jnp.where(numbers == chosen, scores, 0.0), axis=0, keepdims=True)
        new_top = jnp.maximum(top, jnp.max(scores, axis=0, keepdims=True))
        mass = mass * jnp.exp(top - new_top) + jnp.sum(
            jnp.exp(scores - new_top), axis=0, keepdims=True
        )
        return new_top, mass, picked

    zero = jnp.zeros((1, count), jnp.float32)
    top, mass, picked = lax.fori_loop(
        0, old_rows // tile, old_tile, (jnp.full((1, count), -jnp.inf, jnp.float32), zero, zero)
    )

    pooled = part[n]
    for k in range(1, narrow_count):
        other = lax.rem(n + k, narrow_count)
        part_copy(other, n).wait_recv()
        pooled += part_in[other]
    square = jnp.sum(pooled * pooled, axis=1, keepdims=True)
    square = sum(square[g * per : (g + 1) * per] for g in range(groups)) * (1.0 / width)
    norm = lax.rsqrt(jnp.concatenate([square] * groups, axis=0) + EPS)
    folded = (pooled * norm * out_gain_ref[...]).astype(jnp.bfloat16).astype(jnp.float32)
    rows = jnp.concatenate([folded[g * per : (g + 1) * per] for g in range(groups)], axis=1)
    rows = jnp.concatenate([rows, jnp.zeros((MSG - per, width), jnp.float32)], axis=0)

    piece = width // SPLIT
    spread = jnp.concatenate([rows[:8, j * piece : (j + 1) * piece] for j in range(SPLIT)], axis=0)
    outgoing = jnp.dot(place_ref[...], spread.astype(jnp.bfloat16), preferred_element_type=jnp.float32)
    messages[...] = outgoing.astype(jnp.bfloat16).reshape(wide_count, MSG, piece)
    holder = w // sources
    slot = lax.rem(w, sources) * narrow_count + n

    def message_copy(target, at):
        return pltpu.make_async_remote_copy(
            src_ref=messages.at[target],
            dst_ref=messages_in.at[at],
            send_sem=msg_send.at[target],
            recv_sem=msg_recv.at[at],
            device_id=(target, holder),
            device_id_type=MESH,
        )

    local_message = pltpu.make_async_copy(
        messages.at[w], messages_in.at[slot], own_sem.at[2]
    )

    @pl.loop(1, wide_count)
    def _(k):
        message_copy(lax.rem(w + k, wide_count), slot).start()

    @pl.when(holder == n)
    def _():
        local_message.start()

    @pl.when(holder != n)
    def _():
        message_copy(w, slot).start()

    scores = factor * lax.dot_general(
        rows.astype(jnp.bfloat16), blocks[...], contract, preferred_element_type=jnp.float32
    )
    place = lax.broadcasted_iota(jnp.int32, (MSG, 1), 0)
    valid = place < per
    numbers = devices * old_rows + w * passages + n * per + place
    picked += jnp.sum(jnp.where(valid & (numbers == chosen), scores, 0.0), axis=0, keepdims=True)
    masked = jnp.where(valid, scores, -jnp.inf)
    new_top = jnp.maximum(top, jnp.max(masked, axis=0, keepdims=True))
    mass = mass * jnp.exp(top - new_top) + jnp.sum(
        jnp.exp(masked - new_top), axis=0, keepdims=True
    )
    halves = count // 128
    stat = [v[:, h * 128 : (h + 1) * 128] for v in (new_top, mass, picked) for h in range(halves)]
    stat.append(jnp.zeros((8 - 3 * halves, 128), jnp.float32))
    stats[me] = jnp.concatenate(stat, axis=0)

    def stat_copy(sender, target):
        return pltpu.make_async_remote_copy(
            src_ref=stats.at[sender],
            dst_ref=stats.at[sender],
            send_sem=stat_send.at[target],
            recv_sem=stat_recv.at[sender],
            device_id=(target // narrow_count, lax.rem(target, narrow_count)),
            device_id_type=MESH,
        )

    @pl.loop(1, devices)
    def _(k):
        stat_copy(me, lax.rem(me + k, devices)).start()

    @pl.loop(0, sources)
    def _(a):
        @pl.loop(0, narrow_count)
        def _(b):
            at = a * narrow_count + b

            @pl.when((n * sources + a == w) & (b == n))
            def _():
                local_message.wait()

            @pl.when((n * sources + a != w) | (b != n))
            def _():
                message_copy(w, at).wait_recv()

    for a in range(sources):
        held = messages_in[a * narrow_count].astype(jnp.float32)
        for b in range(1, narrow_count):
            held += messages_in[a * narrow_count + b].astype(jnp.float32)
        index_ref[a] = held.astype(jnp.bfloat16)

    @pl.loop(1, devices)
    def _(k):
        stat_copy(lax.rem(me + k, devices), me).wait_recv()

    every = stats[...]
    tops = every[:, :halves, :]
    largest = jnp.max(tops, axis=0)
    masses = jnp.sum(every[:, halves : 2 * halves, :] * jnp.exp(tops - largest[None]), axis=0)
    chosen_score = jnp.sum(every[:, 2 * halves : 3 * halves, :], axis=0)
    losses_ref[...] = largest + jnp.log(masses) - chosen_score

    @pl.loop(1, wide_count)
    def _(k):
        target = lax.rem(w + k, wide_count)
        for copy in query_copies(w, target):
            copy.wait_send()
        message_copy(target, slot).wait_send()

    @pl.when(holder != n)
    def _():
        message_copy(w, slot).wait_send()

    for k in range(1, narrow_count):
        part_copy(n, lax.rem(n + k, narrow_count)).wait_send()

    @pl.loop(1, devices)
    def _(k):
        stat_copy(me, lax.rem(me + k, devices)).wait_send()


def local(
    tokens,
    ln_gain,
    gate_weight,
    up_weight,
    down_weight,
    out_gain,
    shard_ids,
    slab_old,
    queries,
    positives,
    owners,
):
    passages, seq, width = tokens.shape
    narrow_count = lax.axis_size("narrow")
    wide_count = lax.axis_size("wide")
    narrow_rank = lax.axis_index("narrow")
    units = gate_weight.shape[1]
    steps, block = owners.shape[0], queries.shape[1]
    count = steps * block
    per = passages // narrow_count
    capacity = 2 * passages // wide_count
    sources = wide_count // narrow_count
    devices = wide_count * narrow_count
    groups = 8 // per
    lanes = width // groups
    piece = width // SPLIT
    chunks = -(-units // CHUNK)

    positions = jnp.arange(passages, dtype=jnp.int32)
    earlier = positions[:, None] > positions[None, :]
    same = shard_ids[:, None] == shard_ids[None, :]
    rank = jnp.sum((earlier & same).astype(jnp.int32), axis=1)
    slots = shard_ids * capacity + rank
    own = lax.dynamic_slice_in_dim(slots, narrow_rank * per, per, 0)
    own = jnp.concatenate([own, jnp.full((8 - per,), -1, jnp.int32)])
    row = jnp.arange(wide_count * MSG, dtype=jnp.int32)[:, None]
    shard, inner = row // MSG, row % MSG
    column = jnp.arange(SPLIT * 8, dtype=jnp.int32)[None, :]
    place = (
        (inner < SPLIT * capacity)
        & (inner // capacity == column // 8)
        & (jnp.tile(own, SPLIT)[None, :] == shard * capacity + inner % capacity)
    ).astype(jnp.bfloat16)

    gain_out = jnp.repeat(out_gain.astype(jnp.float32).reshape(groups, lanes), per, axis=0)
    paired = jnp.broadcast_to(jnp.concatenate([positives, positives], axis=1), (8, 2 * block))

    vmem = pl.BlockSpec(memory_space=pltpu.VMEM)
    anywhere = pl.BlockSpec(memory_space=pl.ANY)
    dma = pltpu.SemaphoreType.DMA
    flops = 4 * passages * seq * width * units + 2 * count * width * slab_old.shape[0]
    moved = 2 * width * (passages * seq + 3 * units + slab_old.shape[0])
    index_part, losses = pl.pallas_call(
        functools.partial(kernel, (passages, seq, wide_count, narrow_count, steps, block)),
        out_shape=(
            jax.ShapeDtypeStruct((sources, MSG, piece), jnp.bfloat16),
            jax.ShapeDtypeStruct((count // 128, 128), jnp.float32),
        ),
        in_specs=[
            anywhere,
            vmem,
            anywhere,
            anywhere,
            anywhere,
            vmem,
            vmem,
            anywhere,
            anywhere,
            vmem,
            pl.BlockSpec(memory_space=pltpu.SMEM),
        ],
        out_specs=(vmem, vmem),
        scratch_shapes=[
            pltpu.VMEM((passages * seq, width), jnp.bfloat16),
            pltpu.VMEM((width, units), jnp.bfloat16),
            pltpu.VMEM((width, units), jnp.bfloat16),
            pltpu.VMEM((units, width), jnp.bfloat16),
            pltpu.VMEM(slab_old.shape, jnp.bfloat16),
            pltpu.VMEM((wide_count, block, width), jnp.bfloat16),
            pltpu.VMEM((wide_count, 8, 2 * block), jnp.int32),
            pltpu.VMEM((count, width), jnp.bfloat16),
            pltpu.VMEM((chunks, passages, CHUNK), jnp.float32),
            pltpu.VMEM((passages, width), jnp.float32),
            pltpu.VMEM((2 * passages, width), jnp.float32),
            pltpu.VMEM((narrow_count, 8, lanes), jnp.float32),
            pltpu.VMEM((narrow_count, 8, lanes), jnp.float32),
            pltpu.VMEM((wide_count, MSG, piece), jnp.bfloat16),
            pltpu.VMEM((sources * narrow_count, MSG, piece), jnp.bfloat16),
            pltpu.VMEM((devices, 8, 128), jnp.float32),
            dma((passages,)),
            dma((2, LOADS)),
            dma((2,)),
            dma((3,)),
            dma((wide_count,)),
            dma((wide_count,)),
            dma((wide_count,)),
            dma((wide_count,)),
            dma((narrow_count,)),
            dma((narrow_count,)),
            dma((wide_count,)),
            dma((sources * narrow_count,)),
            dma((devices,)),
            dma((devices,)),
        ],
        compiler_params=pltpu.CompilerParams(
            collective_id=0, has_side_effects=True, vmem_limit_bytes=58 * 1024 * 1024
        ),
        cost_estimate=pl.CostEstimate(
            flops=flops, bytes_accessed=moved, transcendentals=passages * seq * units
        ),
    )(
        tokens.reshape(passages * seq, width),
        ln_gain.astype(jnp.float32).reshape(1, width),
        gate_weight,
        up_weight,
        down_weight,
        gain_out,
        place,
        slab_old,
        queries[0],
        paired,
        owners,
    )
    arrived = index_part[:, : SPLIT * capacity].reshape(sources, SPLIT, capacity, piece)
    arrived = arrived.transpose(0, 2, 1, 3).reshape(1, sources, capacity, width)
    return arrived, losses.reshape(steps, block)


def solution(mesh):
    return jax.shard_map(
        local,
        mesh=mesh,
        in_specs=(
            P("wide", None, None),
            P(),
            P(None, "narrow"),
            P(None, "narrow"),
            P("narrow", None),
            P(),
            P("wide"),
            P(("wide", "narrow"), None),
            P("wide", None, None),
            P("wide", None),
            P(),
        ),
        out_specs=(P("wide", "narrow", None, None), P()),
        check_vma=False,
    )
```

time: 261 us -> 88.7 us (0.34)
  blocking collectives: 132 us -> 0 us
  matrix products: 63.3 us -> 0 us
  Pallas kernels: 0 us -> 58.9 us
  local copies, waits for them, and re-layouts: 5.57 us -> 25.2 us
  starting transfers between devices: 17.3 us -> 0 us
  waiting for transfers between devices: 15.5 us -> 0 us
  between operations: 14.2 us -> 0.66 us
  other arithmetic: 11.8 us -> 3.11 us
    psum x2 -> x0, blocking collectives: 93.9 us -> none  [the longest x1 54.1 us: local(): lax.psum((own_blocks, own_positives), 'wide')]
    dot_general x5 -> x0, matrix products: 63.3 us -> none  [the longest x1 39.4 us: local(): jnp.dot(hidden, down_weight, preferred_element_type=jnp.float32)]
    pallas_call x0 -> x1, Pallas kernels: none -> 58.9 us  [local(): pl.pallas_call(functools.partial(kernel, (passages, seq, wide_count, narr...]
    pmax x1 -> x0, blocking collectives: 38.4 us -> none  [local(): largest = lax.pmax(local_max, ('wide', 'narrow'))]
    all_to_all x4 -> x0, starting transfers between devices: 17.2 us -> none  [the longest x1 5.18 us: local(): lax.all_to_all(slot_numbers, 'wide', split_axis=0, concat_axis=0, tiled=T...]
    unnamed x15 -> x2, local copies, waits for them, and re-layouts: 2.63 us -> 19.2 us
    all_to_all x4 -> x0, waiting for transfers between devices: 15.4 us -> none  [the longest x1 5.49 us: local(): lax.all_to_all(lax.all_to_all(slot_numbers, 'wide', split_axis=0, concat_...]
    reduce_sum x5 -> x0, other arithmetic: 7.22 us -> none  [the longest x1 5.4 us: local(): token_mean = jnp.mean(values, axis=1)]
  transfers between devices with their start and end apart: 5 -> 0, of which waited for: 3 -> 0; matrix products, arithmetic and copies ran while one was open for 3% -> 0% of each run, Pallas kernels for 0% -> 0%
where the time goes in v1:
time: 88.7 us; the launch traced here: 87.9 us
  Pallas kernels  58.9 us (66%)
  local copies, waits for them, and re-layouts  25.2 us (28%)
  other arithmetic  3.11 us (4%)
    pallas_call x1, Pallas kernels, local(): pl.pallas_call(functools.partial(kernel, (passages, seq, wide_count, narr...  58.9 us
    unnamed x2, local copies, waits for them, and re-layouts  19.2 us

profile of v1, /device:TPU:0, one launch (start us, length us, event | category | flops | bytes accessed | tf_op | source)
XLA Modules:
  0.0 87.9 jit_solution(17535585941805407647)
XLA Ops:
  0.6 0.8 add_bitcast_fusion
  1.4 0.9 %convert_reduce_fusion = s32[16]{0:T(128)S(1)} fusion(s32[16]{0:T(128)} %param.17), kind=kLoop, calls=%fused_computation.1 | loop fusion | flops 1264 | bytes 128 | tf_op jit(solution)/shard_map/reduce_sum | solution.py:426
  2.4 0.7 multiply_add_fusion
  3.0 0.1 dynamic_slice.3
  3.1 0.1 eq.50
  3.2 0.6 broadcast_in_dim.8.positives_ref
  3.8 1.3 %reshape.190.gain_ref = f32[1,1536]{1,0:T(1,128)} reshape(bf16[1536]{0:T(1024)(128)(2,1)} %param.12) | data formatting | bytes 9216 | tf_op jit(solution)/shard_map/reshape | solution.py:507
  5.1 0.7 reshape.192
  5.8 0.6 reshape.185.out_gain_ref
  6.4 0.7 and_convert_fusion.place_ref
  7.1 9.6 %copy.20.gate_ref = bf16[1536,2240]{1,0:T(8,128)(2,1)} copy(bf16[1536,2240]{0,1:T(8,128)(2,1)} %param.13) | data formatting | bytes 13762560 | tf_op args[2]
  16.7 9.6 %copy.21.up_ref = bf16[1536,2240]{1,0:T(8,128)(2,1)} copy(bf16[1536,2240]{0,1:T(8,128)(2,1)} %param.14) | data formatting | bytes 13762560 | tf_op args[3]
  26.3 58.9 %shard_map.122 = (bf16[2,16,384]{2,1,0:T(8,128)(2,1)}, f32[2,128]{1,0:T(2,128)}) custom-call(bf16[2048,1536]{1,0:T(8,128)(2,1)} %bitcast.8, f32[1,1536]{1,0:T(1,128)} %reshape.190.gain_ref, bf16[1536,2240]{1,0:T(8,128)(2,1)} %copy.20.gate_ref, bf16[1536,2240]{1,0:T(8,128)(2,1)} %copy.21.up_ref, bf16[2240,1536]{1,0:T(8,128)(2,1)} %down_ref.1, ...), custom_call_target="tpu_custom_call" | custom-call | flops 29796335616 | bytes 33226752 | tf_op jit(solution)/shard_map/pallas_call | solution.py:447
  85.2 1.4 %reshape.186 = bf16[2,4,4,384]{3,2,1,0:T(4,128)(2,1)} reshape(bf16[2,16,384]{2,1,0:T(8,128)(2,1)} %get-tuple-element.4) | data formatting | bytes 49152 | tf_op jit(solution)/shard_map/reshape | solution.py:518
  86.5 1.3 %reshape.188 = f32[4,64]{1,0:T(4,128)} reshape(f32[2,128]{1,0:T(2,128)} %get-tuple-element.5) | data formatting | bytes 2048 | tf_op jit(solution)/shard_map/reshape | solution.py:520
  (6 shorter events, 0.0 us)

commit v2 on v1

--- a/solution.py
+++ b/solution.py
@@ -11,21 +11,19 @@
 EPS = 1e-06
 MESH = pl.DeviceIdType.MESH
 CHUNK = 256
-ROWS = 256
+ROWS = 512
 SPLIT = 4
-LOADS = 4
 MSG = 16
 
 
 def kernel(
     dims,
     tokens_ref,
-    gain_ref,
+    gains_ref,
     gate_ref,
     up_ref,
     down_ref,
-    out_gain_ref,
-    place_ref,
+    shards_ref,
     slab_ref,
     queries_ref,
     positives_ref,
@@ -38,6 +36,7 @@
     down_v,
     slab_v,
     q_all,
+    p_own,
     p_all,
     blocks,
     hidden_sum,
@@ -65,7 +64,8 @@
 ):
     passages, seq, wide_count, narrow_count, steps, block = dims
     width = tokens_ref.shape[1]
-    units = gate_ref.shape[1]
+    units = gate_ref.shape[0]
+    capacity = index_ref.shape[1]
     full, tail = units // CHUNK, units % CHUNK
     per = passages // narrow_count
     groups = 8 // per
@@ -81,8 +81,8 @@
         rows = pl.ds(pl.multiple_of(i * seq, seq), seq)
         return pltpu.make_async_copy(tokens_ref.at[rows, :], x_ref.at[rows, :], x_sem.at[i])
 
-    def weight_copies(c):
-        rows = pl.ds(pl.multiple_of(c * (width // LOADS), width // LOADS), width // LOADS)
+    def weight_copies(c, size):
+        rows = pl.ds(pl.multiple_of(c * CHUNK, CHUNK), size)
         return (
             pltpu.make_async_copy(gate_ref.at[rows, :], gate_v.at[rows, :], w_sem.at[0, c]),
             pltpu.make_async_copy(up_ref.at[rows, :], up_v.at[rows, :], w_sem.at[1, c]),
@@ -91,21 +91,22 @@
     down_copy = pltpu.make_async_copy(down_ref, down_v, big_sem.at[0])
     slab_copy = pltpu.make_async_copy(slab_ref, slab_v, big_sem.at[1])
     own_q = pltpu.make_async_copy(queries_ref, q_all.at[w], own_sem.at[0])
-    own_p = pltpu.make_async_copy(positives_ref, p_all.at[w], own_sem.at[1])
 
     @pl.loop(0, passages)
     def _(i):
         token_copy(i).start()
 
-    @pl.loop(0, LOADS)
+    @pl.loop(0, full)
     def _(c):
-        for copy in weight_copies(c):
+        for copy in weight_copies(c, CHUNK):
             copy.start()
 
+    if tail:
+        for copy in weight_copies(full, tail):
+            copy.start()
     down_copy.start()
     slab_copy.start()
     own_q.start()
-    own_p.start()
 
     barrier = pltpu.get_barrier_semaphore()
 
@@ -119,7 +120,11 @@
             device_id_type=MESH,
         )
 
-    gain = gain_ref[...]
+    gain = gains_ref[0:1, :]
+    p_own[...] = jnp.zeros_like(p_own)
+    p_own[0:1, :block] = positives_ref[...]
+    p_own[0:1, block:] = positives_ref[...]
+    p_all[w] = p_own[...]
 
     @pl.loop(0, passages)
     def _(i):
@@ -143,7 +148,7 @@
                 device_id_type=MESH,
             ),
             pltpu.make_async_remote_copy(
-                src_ref=positives_ref,
+                src_ref=p_own,
                 dst_ref=p_all.at[owner],
                 send_sem=p_send.at[target],
                 recv_sem=p_recv.at[owner],
@@ -157,13 +162,15 @@
         for copy in query_copies(w, lax.rem(w + k, wide_count)):
             copy.start()
 
+    contract = (((1,), (1,)), ((), ()))
+
     def encode(c, size):
-        cols = pl.ds(pl.multiple_of(c * CHUNK, CHUNK), size)
+        units_of = pl.ds(pl.multiple_of(c * CHUNK, CHUNK), size)
         held = ROWS // seq
         for i in range(passages // held):
             x = x_ref[i * ROWS : (i + 1) * ROWS, :]
-            gate = jnp.dot(x, gate_v[:, cols], preferred_element_type=jnp.float32)
-            upward = jnp.dot(x, up_v[:, cols], preferred_element_type=jnp.float32)
+            gate = lax.dot_general(x, gate_v[units_of, :], contract, preferred_element_type=jnp.float32)
+            upward = lax.dot_general(x, up_v[units_of, :], contract, preferred_element_type=jnp.float32)
             hidden = gate * upward * (1.0 + jnp.tanh(0.5 * gate))
             summed = jnp.sum(hidden.reshape(held, seq, size), axis=1)
             hidden_sum[c, i * held : (i + 1) * held, :size] = summed * (0.5 / seq)
@@ -181,21 +188,22 @@
 
     total[...] = jnp.zeros_like(total)
 
-    @pl.loop(0, LOADS)
-    def _(c):
-        for copy in weight_copies(c):
-            copy.wait()
-
+    for copy in weight_copies(0, CHUNK):
+        copy.wait()
     encode(0, CHUNK)
     down_copy.wait()
 
     @pl.loop(1, full)
     def _(c):
+        for copy in weight_copies(c, CHUNK):
+            copy.wait()
         project(c - 1, CHUNK)
         encode(c, CHUNK)
 
     project(full - 1, CHUNK)
     if tail:
+        for copy in weight_copies(full, tail):
+            copy.wait()
         encode(full, tail)
         project(full, tail)
 
@@ -220,7 +228,6 @@
         part_copy(n, lax.rem(n + k, narrow_count)).start()
 
     own_q.wait()
-    own_p.wait()
 
     @pl.loop(1, wide_count)
     def _(k):
@@ -241,7 +248,6 @@
         )
     chosen = jnp.concatenate(pieces, axis=1)
     factor = 1.0 / math.sqrt(width)
-    contract = (((1,), (1,)), ((), ()))
     slab_copy.wait()
     old_rows = slab_ref.shape[0]
     tile = 512
@@ -265,21 +271,44 @@
         0, old_rows // tile, old_tile, (jnp.full((1, count), -jnp.inf, jnp.float32), zero, zero)
     )
 
+    row = lax.broadcasted_iota(jnp.int32, (wide_count * MSG, SPLIT * 8), 0)
+    column = lax.broadcasted_iota(jnp.int32, (wide_count * MSG, SPLIT * 8), 1)
+    inner = row % MSG
+    wanted = (row // MSG) * capacity + inner % capacity
+    lined = (inner < SPLIT * capacity) & (inner // capacity == column // 8)
+    place = jnp.zeros((wide_count * MSG, SPLIT * 8), jnp.float32)
+    for p in range(per):
+        at = n * per + p
+        shard = shards_ref[at]
+        rank = 0
+        for q in range(passages):
+            rank += jnp.where((q < at) & (shards_ref[q] == shard), 1, 0)
+        hit = lined & (column % 8 == p) & (wanted == shard * capacity + rank)
+        place = jnp.where(hit, 1.0, place)
+    place = place.astype(jnp.bfloat16)
+
     pooled = part[n]
     for k in range(1, narrow_count):
         other = lax.rem(n + k, narrow_count)
         part_copy(other, n).wait_recv()
         pooled += part_in[other]
+    gain_out = jnp.concatenate(
+        [
+            jnp.broadcast_to(gains_ref[1:2, g * lanes : (g + 1) * lanes], (per, lanes))
+            for g in range(groups)
+        ],
+        axis=0,
+    )
     square = jnp.sum(pooled * pooled, axis=1, keepdims=True)
     square = sum(square[g * per : (g + 1) * per] for g in range(groups)) * (1.0 / width)
     norm = lax.rsqrt(jnp.concatenate([square] * groups, axis=0) + EPS)
-    folded = (pooled * norm * out_gain_ref[...]).astype(jnp.bfloat16).astype(jnp.float32)
+    folded = (pooled * norm * gain_out).astype(jnp.bfloat16).astype(jnp.float32)
     rows = jnp.concatenate([folded[g * per : (g + 1) * per] for g in range(groups)], axis=1)
     rows = jnp.concatenate([rows, jnp.zeros((MSG - per, width), jnp.float32)], axis=0)
 
     piece = width // SPLIT
     spread = jnp.concatenate([rows[:8, j * piece : (j + 1) * piece] for j in range(SPLIT)], axis=0)
-    outgoing = jnp.dot(place_ref[...], spread.astype(jnp.bfloat16), preferred_element_type=jnp.float32)
+    outgoing = jnp.dot(place, spread.astype(jnp.bfloat16), preferred_element_type=jnp.float32)
     messages[...] = outgoing.astype(jnp.bfloat16).reshape(wide_count, MSG, piece)
     holder = w // sources
     slot = lax.rem(w, sources) * narrow_count + n
@@ -313,9 +342,9 @@
     scores = factor * lax.dot_general(
         rows.astype(jnp.bfloat16), blocks[...], contract, preferred_element_type=jnp.float32
     )
-    place = lax.broadcasted_iota(jnp.int32, (MSG, 1), 0)
-    valid = place < per
-    numbers = devices * old_rows + w * passages + n * per + place
+    spot = lax.broadcasted_iota(jnp.int32, (MSG, 1), 0)
+    valid = spot < per
+    numbers = devices * old_rows + w * passages + n * per + spot
     picked += jnp.sum(jnp.where(valid & (numbers == chosen), scores, 0.0), axis=0, keepdims=True)
     masked = jnp.where(valid, scores, -jnp.inf)
     new_top = jnp.maximum(top, jnp.max(masked, axis=0, keepdims=True))
@@ -359,7 +388,9 @@
         held = messages_in[a * narrow_count].astype(jnp.float32)
         for b in range(1, narrow_count):
             held += messages_in[a * narrow_count + b].astype(jnp.float32)
-        index_ref[a] = held.astype(jnp.bfloat16)
+        index_ref[a] = jnp.concatenate(
+            [held[j * capacity : (j + 1) * capacity] for j in range(SPLIT)], axis=1
+        ).astype(jnp.bfloat16)
 
     @pl.loop(1, devices)
     def _(k):
@@ -370,7 +401,10 @@
     largest = jnp.max(tops, axis=0)
     masses = jnp.sum(every[:, halves : 2 * halves, :] * jnp.exp(tops - largest[None]), axis=0)
     chosen_score = jnp.sum(every[:, 2 * halves : 3 * halves, :], axis=0)
-    losses_ref[...] = largest + jnp.log(masses) - chosen_score
+    loss = largest + jnp.log(masses) - chosen_score
+    for t in range(steps):
+        side = t % 2 * block
+        losses_ref[t : t + 1, :] = loss[t // 2 : t // 2 + 1, side : side + block]
 
     @pl.loop(1, wide_count)
     def _(k):
@@ -407,7 +441,6 @@
     passages, seq, width = tokens.shape
     narrow_count = lax.axis_size("narrow")
     wide_count = lax.axis_size("wide")
-    narrow_rank = lax.axis_index("narrow")
     units = gate_weight.shape[1]
     steps, block = owners.shape[0], queries.shape[1]
     count = steps * block
@@ -420,35 +453,18 @@
     piece = width // SPLIT
     chunks = -(-units // CHUNK)
 
-    positions = jnp.arange(passages, dtype=jnp.int32)
-    earlier = positions[:, None] > positions[None, :]
-    same = shard_ids[:, None] == shard_ids[None, :]
-    rank = jnp.sum((earlier & same).astype(jnp.int32), axis=1)
-    slots = shard_ids * capacity + rank
-    own = lax.dynamic_slice_in_dim(slots, narrow_rank * per, per, 0)
-    own = jnp.concatenate([own, jnp.full((8 - per,), -1, jnp.int32)])
-    row = jnp.arange(wide_count * MSG, dtype=jnp.int32)[:, None]
-    shard, inner = row // MSG, row % MSG
-    column = jnp.arange(SPLIT * 8, dtype=jnp.int32)[None, :]
-    place = (
-        (inner < SPLIT * capacity)
-        & (inner // capacity == column // 8)
-        & (jnp.tile(own, SPLIT)[None, :] == shard * capacity + inner % capacity)
-    ).astype(jnp.bfloat16)
-
-    gain_out = jnp.repeat(out_gain.astype(jnp.float32).reshape(groups, lanes), per, axis=0)
-    paired = jnp.broadcast_to(jnp.concatenate([positives, positives], axis=1), (8, 2 * block))
-
+    gains = jnp.stack([ln_gain, out_gain]).astype(jnp.float32)
     vmem = pl.BlockSpec(memory_space=pltpu.VMEM)
     anywhere = pl.BlockSpec(memory_space=pl.ANY)
+    smem = pl.BlockSpec(memory_space=pltpu.SMEM)
     dma = pltpu.SemaphoreType.DMA
     flops = 4 * passages * seq * width * units + 2 * count * width * slab_old.shape[0]
     moved = 2 * width * (passages * seq + 3 * units + slab_old.shape[0])
     index_part, losses = pl.pallas_call(
         functools.partial(kernel, (passages, seq, wide_count, narrow_count, steps, block)),
         out_shape=(
-            jax.ShapeDtypeStruct((sources, MSG, piece), jnp.bfloat16),
-            jax.ShapeDtypeStruct((count // 128, 128), jnp.float32),
+            jax.ShapeDtypeStruct((sources, capacity, width), jnp.bfloat16),
+            jax.ShapeDtypeStruct((steps, block), jnp.float32),
         ),
         in_specs=[
             anywhere,
@@ -456,21 +472,21 @@
             anywhere,
             anywhere,
             anywhere,
-            vmem,
-            vmem,
+            smem,
             anywhere,
             anywhere,
             vmem,
-            pl.BlockSpec(memory_space=pltpu.SMEM),
+            smem,
         ],
         out_specs=(vmem, vmem),
         scratch_shapes=[
             pltpu.VMEM((passages * seq, width), jnp.bfloat16),
-            pltpu.VMEM((width, units), jnp.bfloat16),
-            pltpu.VMEM((width, units), jnp.bfloat16),
+            pltpu.VMEM((units, width), jnp.bfloat16),
+            pltpu.VMEM((units, width), jnp.bfloat16),
             pltpu.VMEM((units, width), jnp.bfloat16),
             pltpu.VMEM(slab_old.shape, jnp.bfloat16),
             pltpu.VMEM((wide_count, block, width), jnp.bfloat16),
+            pltpu.VMEM((8, 2 * block), jnp.int32),
             pltpu.VMEM((wide_count, 8, 2 * block), jnp.int32),
             pltpu.VMEM((count, width), jnp.bfloat16),
             pltpu.VMEM((chunks, passages, CHUNK), jnp.float32),
@@ -482,7 +498,7 @@
             pltpu.VMEM((sources * narrow_count, MSG, piece), jnp.bfloat16),
             pltpu.VMEM((devices, 8, 128), jnp.float32),
             dma((passages,)),
-            dma((2, LOADS)),
+            dma((2, chunks)),
             dma((2,)),
             dma((3,)),
             dma((wide_count,)),
@@ -504,20 +520,17 @@
         ),
     )(
         tokens.reshape(passages * seq, width),
-        ln_gain.astype(jnp.float32).reshape(1, width),
-        gate_weight,
-        up_weight,
+        gains,
+        gate_weight.T,
+        up_weight.T,
         down_weight,
-        gain_out,
-        place,
+        shard_ids,
         slab_old,
         queries[0],
-        paired,
+        positives,
         owners,
     )
-    arrived = index_part[:, : SPLIT * capacity].reshape(sources, SPLIT, capacity, piece)
-    arrived = arrived.transpose(0, 2, 1, 3).reshape(1, sources, capacity, width)
-    return arrived, losses.reshape(steps, block)
+    return index_part[None], losses
 
 
 def solution(mesh):

time: 88.7 us -> 63.3 us (0.71)
  local copies, waits for them, and re-layouts: 25.2 us -> 3.98 us
  other arithmetic: 3.11 us -> 0.62 us
  Pallas kernels: 58.9 us -> 57.8 us
    unnamed x2, local copies, waits for them, and re-layouts: 19.2 us -> 2.6 us
    reshape x5 -> x0, local copies, waits for them, and re-layouts: 5.3 us -> none  [the longest x1 1.36 us: local(): index_part[:, :SPLIT * capacity].reshape(sources, SPLIT, capacity, piece)]
    another operation x1 -> x2, local copies, waits for them, and re-layouts: 0.01 us -> 1.38 us  [local(): gains = jnp.stack([ln_gain, out_gain]).astype(jnp.float32)]
    pallas_call x1, Pallas kernels: 58.9 us -> 57.8 us  [local(): pl.pallas_call(functools.partial(kernel, (passages, seq, wide_count, narr...]
    reduce_sum x1 -> x0, other arithmetic: 0.91 us -> none  [local(): rank = jnp.sum((earlier & same).astype(jnp.int32), axis=1)]
where the time goes in v2:
time: 63.3 us; the launch traced here: 63 us
  Pallas kernels  57.8 us (91%)
  local copies, waits for them, and re-layouts  3.98 us (6%)
  between operations  0.64 us (1%)
    pallas_call x1, Pallas kernels, local(): pl.pallas_call(functools.partial(kernel, (passages, seq, wide_count, narr...  57.8 us
    unnamed x2, local copies, waits for them, and re-layouts  2.6 us
    another operation x2, local copies, waits for them, and re-layouts, local(): gains = jnp.stack([ln_gain, out_gain]).astype(jnp.float32)  1.38 us

profile of v2, /device:TPU:0, one launch (start us, length us, event | category | flops | bytes accessed | tf_op | source)
XLA Modules:
  0.0 63.0 jit_solution(13215648557855295274)
XLA Ops:
  0.6 0.7 %stack.9 = bf16[1,1536]{1,0:T(2,128)(2,1)S(1)} reshape(bf16[1536]{0:T(1024)(128)(2,1)} %param.12) | data formatting | bytes 6144 | tf_op jit(solution)/shard_map/stack | solution.py:456
  1.3 0.7 %stack.10 = bf16[1,1536]{1,0:T(2,128)(2,1)S(1)} reshape(bf16[1536]{0:T(1024)(128)(2,1)} %param.16) | data formatting | bytes 6144 | tf_op jit(solution)/shard_map/stack | solution.py:456
  2.0 0.6 maximum_convert_fusion.gains_ref
  2.6 57.8 %shard_map.122 = (bf16[2,4,1536]{2,1,0:T(4,128)(2,1)}, f32[4,64]{1,0:T(4,128)}) custom-call(bf16[2048,1536]{1,0:T(8,128)(2,1)} %bitcast.8, f32[2,1536]{1,0:T(2,128)} %maximum_convert_fusion.gains_ref, bf16[2240,1536]{1,0:T(8,128)(2,1)} %bitcast.6, bf16[2240,1536]{1,0:T(8,128)(2,1)} %bitcast.7, bf16[2240,1536]{1,0:T(8,128)(2,1)} %down_ref.1, s32[16]{0:T(128)} %shards_ref.1, ...), custom_call_target="tpu_custom_call" | custom-call | flops 29796335616 | bytes 33226752 | tf_op jit(solution)/shard_map/pallas_call | solution.py:463
  60.4 1.4 %copy.15 = bf16[1,2,4,1536]{3,2,1,0:T(4,128)(2,1)} copy(bf16[1,2,4,1536]{3,2,1,0:T(4,128)(2,1)} %bitcast.5) | data formatting | bytes 49152
  61.8 1.2 %copy.16 = f32[4,64]{1,0:T(4,128)} copy(f32[4,64]{1,0:T(4,128)} %get-tuple-element.9) | data formatting | bytes 2048

commit v3 on v2

--- a/solution.py
+++ b/solution.py
@@ -19,7 +19,8 @@
 def kernel(
     dims,
     tokens_ref,
-    gains_ref,
+    ln_gain_ref,
+    out_gain_ref,
     gate_ref,
     up_ref,
     down_ref,
@@ -120,21 +121,25 @@
             device_id_type=MESH,
         )
 
-    gain = gains_ref[0:1, :]
+    gain = ln_gain_ref[...].astype(jnp.float32).reshape(1, width)
     p_own[...] = jnp.zeros_like(p_own)
     p_own[0:1, :block] = positives_ref[...]
     p_own[0:1, block:] = positives_ref[...]
     p_all[w] = p_own[...]
 
-    @pl.loop(0, passages)
-    def _(i):
-        token_copy(i).wait()
-        rows = pl.ds(pl.multiple_of(i * seq, seq), seq)
-        values = x_ref[rows, :].astype(jnp.float32)
-        scale = lax.rsqrt(jnp.mean(values * values, axis=1, keepdims=True) + EPS)
-        token_mean[pl.ds(i, 1), :] = jnp.sum(values, axis=0, keepdims=True) * (1.0 / seq)
-        x_ref[rows, :] = (values * scale * gain).astype(jnp.bfloat16)
-
+    held = ROWS // seq
+
+    def normalize(i):
+        for p in range(i * held, (i + 1) * held):
+            token_copy(p).wait()
+        for p in range(i * held, (i + 1) * held):
+            rows = slice(p * seq, (p + 1) * seq)
+            values = x_ref[rows, :].astype(jnp.float32)
+            scale = lax.rsqrt(jnp.mean(values * values, axis=1, keepdims=True) + EPS)
+            token_mean[p : p + 1, :] = jnp.sum(values, axis=0, keepdims=True) * (1.0 / seq)
+            x_ref[rows, :] = (values * scale * gain).astype(jnp.bfloat16)
+
+    normalize(0)
     pl.semaphore_wait(barrier, devices - 1)
 
     def query_copies(owner, target):
@@ -164,10 +169,11 @@
 
     contract = (((1,), (1,)), ((), ()))
 
-    def encode(c, size):
+    def encode(c, size, first=False):
         units_of = pl.ds(pl.multiple_of(c * CHUNK, CHUNK), size)
-        held = ROWS // seq
         for i in range(passages // held):
+            if first and i + 1 < passages // held:
+                normalize(i + 1)
             x = x_ref[i * ROWS : (i + 1) * ROWS, :]
             gate = lax.dot_general(x, gate_v[units_of, :], contract, preferred_element_type=jnp.float32)
             upward = lax.dot_general(x, up_v[units_of, :], contract, preferred_element_type=jnp.float32)
@@ -190,7 +196,7 @@
 
     for copy in weight_copies(0, CHUNK):
         copy.wait()
-    encode(0, CHUNK)
+    encode(0, CHUNK, True)
     down_copy.wait()
 
     @pl.loop(1, full)
@@ -292,9 +298,10 @@
         other = lax.rem(n + k, narrow_count)
         part_copy(other, n).wait_recv()
         pooled += part_in[other]
+    gain_row = out_gain_ref[...].astype(jnp.float32).reshape(1, width)
     gain_out = jnp.concatenate(
         [
-            jnp.broadcast_to(gains_ref[1:2, g * lanes : (g + 1) * lanes], (per, lanes))
+            jnp.broadcast_to(gain_row[:, g * lanes : (g + 1) * lanes], (per, lanes))
             for g in range(groups)
         ],
         axis=0,
@@ -390,7 +397,7 @@
             held += messages_in[a * narrow_count + b].astype(jnp.float32)
         index_ref[a] = jnp.concatenate(
             [held[j * capacity : (j + 1) * capacity] for j in range(SPLIT)], axis=1
-        ).astype(jnp.bfloat16)
+        )
 
     @pl.loop(1, devices)
     def _(k):
@@ -401,10 +408,11 @@
     largest = jnp.max(tops, axis=0)
     masses = jnp.sum(every[:, halves : 2 * halves, :] * jnp.exp(tops - largest[None]), axis=0)
     chosen_score = jnp.sum(every[:, 2 * halves : 3 * halves, :], axis=0)
-    loss = largest + jnp.log(masses) - chosen_score
+    base = largest - chosen_score
     for t in range(steps):
         side = t % 2 * block
-        losses_ref[t : t + 1, :] = loss[t // 2 : t // 2 + 1, side : side + block]
+        losses_ref[0, t : t + 1, :] = base[t // 2 : t // 2 + 1, side : side + block]
+        losses_ref[1, t : t + 1, :] = masses[t // 2 : t // 2 + 1, side : side + block]
 
     @pl.loop(1, wide_count)
     def _(k):
@@ -453,7 +461,6 @@
     piece = width // SPLIT
     chunks = -(-units // CHUNK)
 
-    gains = jnp.stack([ln_gain, out_gain]).astype(jnp.float32)
     vmem = pl.BlockSpec(memory_space=pltpu.VMEM)
     anywhere = pl.BlockSpec(memory_space=pl.ANY)
     smem = pl.BlockSpec(memory_space=pltpu.SMEM)
@@ -463,11 +470,12 @@
     index_part, losses = pl.pallas_call(
         functools.partial(kernel, (passages, seq, wide_count, narrow_count, steps, block)),
         out_shape=(
-            jax.ShapeDtypeStruct((sources, capacity, width), jnp.bfloat16),
-            jax.ShapeDtypeStruct((steps, block), jnp.float32),
+            jax.ShapeDtypeStruct((sources, capacity, width), jnp.float32),
+            jax.ShapeDtypeStruct((2, steps, block), jnp.float32),
         ),
         in_specs=[
             anywhere,
+            vmem,
             vmem,
             anywhere,
             anywhere,
@@ -520,7 +528,8 @@
         ),
     )(
         tokens.reshape(passages * seq, width),
-        gains,
+        ln_gain,
+        out_gain,
         gate_weight.T,
         up_weight.T,
         down_weight,
@@ -530,7 +539,7 @@
         positives,
         owners,
     )
-    return index_part[None], losses
+    return index_part[None].astype(jnp.bfloat16), losses[0] + jnp.log(losses[1])
 
 
 def solution(mesh):

time: 63.3 us -> 63 us (level)
  local copies, waits for them, and re-layouts: 3.98 us -> 0 us
  other arithmetic: 0.62 us -> 2.68 us
  Pallas kernels: 57.8 us -> 59.4 us
    unnamed x2 -> x0, local copies, waits for them, and re-layouts: 2.6 us -> none
    pallas_call x1, Pallas kernels: 57.8 us -> 59.4 us  [local(): pl.pallas_call(functools.partial(kernel, (passages, seq, wide_count, narr...]
    another operation x2 -> x0, local copies, waits for them, and re-layouts: 1.38 us -> none  [local(): gains = jnp.stack([ln_gain, out_gain]).astype(jnp.float32)]
    add x0 -> x1, other arithmetic: none -> 1.26 us  [local(): losses[0] + jnp.log(losses[1])]
    convert_element_type x1, other arithmetic: 0.62 us -> 1.42 us  [local(): index_part[None].astype(jnp.bfloat16)]
where the time goes in v3:
time: 63 us; the launch traced here: 62.8 us
  Pallas kernels  59.4 us (94%)
  other arithmetic  2.68 us (4%)
  between operations  0.64 us (1%)
    pallas_call x1, Pallas kernels, local(): pl.pallas_call(functools.partial(kernel, (passages, seq, wide_count, narr...  59.4 us
    convert_element_type x1, other arithmetic, local(): index_part[None].astype(jnp.bfloat16)  1.42 us
    add x1, other arithmetic, local(): losses[0] + jnp.log(losses[1])  1.26 us

profile of v3, /device:TPU:0, one launch (start us, length us, event | category | flops | bytes accessed | tf_op | source)
XLA Modules:
  0.0 62.8 jit_solution(16959925944040794979)
XLA Ops:
  0.6 59.4 %shard_map.122 = (f32[2,4,1536]{2,1,0:T(4,128)}, f32[2,4,64]{2,1,0:T(4,128)}) custom-call(bf16[2048,1536]{1,0:T(8,128)(2,1)} %bitcast.10, bf16[1536]{0:T(1024)(128)(2,1)} %ln_gain_ref.1, bf16[1536]{0:T(1024)(128)(2,1)} %out_gain_ref.1, bf16[2240,1536]{1,0:T(8,128)(2,1)} %bitcast.8, bf16[2240,1536]{1,0:T(8,128)(2,1)} %bitcast.9, bf16[2240,1536]{1,0:T(8,128)(2,1)} %down_ref.1, ...), custom_call_target="tpu_custom_call" | custom-call | flops 29796335616 | bytes 33226752 | tf_op jit(solution)/shard_map/pallas_call | solution.py:470
  60.1 1.4 %convert_bitcast_fusion = bf16[1,2,4,1536]{3,2,1,0:T(4,128)(2,1)} fusion(f32[2,4,1536]{2,1,0:T(4,128)} %get-tuple-element.4), kind=kLoop, calls=%fused_computation | loop fusion | flops 12288 | bytes 73728 | tf_op jit(solution)/shard_map/convert_element_type | solution.py:542
  61.5 1.3 %add_bitcast_fusion = f32[4,64]{1,0:T(4,128)} fusion(f32[2,4,64]{2,1,0:T(4,128)} %get-tuple-element.5), kind=kLoop, calls=%fused_computation.1 | loop fusion | flops 256 | bytes 3072 | tf_op jit(solution)/shard_map/add | solution.py:542
